TPU v7x, 1024 devices: a whole 4x4x32 slice. The times are simulated.
1024 devices in a mesh: band: 16 (over x, y_lo, core), slab: 64 (over z, y_hi).
Axes of the slice: x: 4, y: 4 (y_hi: 2, y_lo: 2; y = y_hi * 2 + y_lo), z: 32, core: 2. Of those that a mesh axis runs over, the one named last changes fastest.
Arguments:
- orbitals: float32 [64, 128, 128, 128], P('band', 'slab'), may hold values from -6 to 6
- occupations: float32 [64], P('band'), may hold values from 0.1 to 1
- accumulated: float32 [64, 128, 128, 128], P('band', 'slab'), may hold values from -6 to 6
Outputs:
- exchange_terms: float32 [64, 128, 128, 128], P('band', 'slab')
All inputs are finite; a program needn't handle non-finite values.
Results may differ from a plain program's by a relative error of at most 0.00012.
Values sent between devices are 32-bit elements; how exact they have to be, the bound alone decides.
A program may use at most 32 MiB of HBM per device.

v0:
```python
import math

import jax
import jax.numpy as jnp
from jax import lax
from jax.sharding import PartitionSpec as P

HOPS = 3


def shifted(value, axis, steps):
    count = lax.axis_size(axis)
    pairs = [(source, (source + steps) % count) for source in range(count)]
    return lax.ppermute(value, axis, pairs)


def hartley_matrix(extent):
    index = jnp.arange(extent, dtype=jnp.int32)
    product = index[:, None] * index[None, :] % extent
    angle = product.astype(jnp.float32) * (2.0 * math.pi / extent)
    return jnp.cos(angle) + jnp.sin(angle)


def signed_wave(index, extent):
    signed = jnp.where(index < extent // 2, index, index - extent)
    return signed.astype(jnp.float32) * (2.0 * math.pi / extent)


def body(orbitals, occupations, accumulated):
    extent = orbitals.shape[2]
    planes = orbitals.shape[1]
    matrix = hartley_matrix(extent)
    full_index = jnp.arange(extent, dtype=jnp.int32)
    local_index = lax.axis_index("slab") * planes + jnp.arange(planes, dtype=jnp.int32)
    wave_full = signed_wave(full_index, extent)
    wave_local = signed_wave(local_index, extent)
    square = (
        wave_full[:, None, None] ** 2
        + wave_local[None, :, None] ** 2
        + wave_full[None, None, :] ** 2
    )
    screening = 4.0 * math.pi / (square + 0.01) / float(extent**3)
    highest = lax.Precision.HIGHEST

    def transform_inner(values):
        spectra = jnp.einsum("pxyz,zc->pxyc", values, matrix, precision=highest)
        return jnp.einsum("pxyc,yb->pxbc", spectra, matrix, precision=highest)

    leading = orbitals[0]
    leading_occ = occupations[0:1]
    carried = (leading, leading_occ)
    visits = []
    for travel in range(HOPS):
        carried = shifted((carried[0], carried[1]), "band", 1)
        visits.append(carried)
    result = accumulated
    for visitor, visitor_occ in visits:
        potentials_spectra = transform_inner(orbitals * visitor[None])
        columns = jnp.einsum(
            "pxbc,xa->pabc",
            lax.all_to_all(potentials_spectra, "slab", split_axis=2, concat_axis=1, tiled=True),
            matrix,
            precision=highest,
        )
        columns = columns * screening[None]
        columns = jnp.einsum("pabc,ax->pxbc", columns, matrix, precision=highest)
        returned = lax.all_to_all(columns, "slab", split_axis=1, concat_axis=2, tiled=True)
        potential = transform_inner(returned)
        result = result - visitor_occ[0] * visitor[None] * potential
    return result


def solution(mesh):
    in_specs = (P("band", "slab", None, None), P("band"), P("band", "slab", None, None))
    out_specs = P("band", "slab", None, None)
    return jax.shard_map(body, mesh=mesh, in_specs=in_specs, out_specs=out_specs, check_vma=False)
```

profile of v0, /device:TPU:1, one launch (start us, length us, event | category | flops | bytes accessed | tf_op | source)
XLA Modules:
  0.0 458.3 jit_solution(6493517577568117822)
XLA Ops:
  0.0 0.9 slice_bitcast_fusion
  0.9 4.6 %collective-permute-start.1 = (f32[2,128,128]{2,1,0:T(8,128)S(1)}, f32[2,128,128]{2,1,0:T(8,128)S(1)}, u32[]{:S(2)}, u32[]{:S(2)}) collective-permute-start(f32[2,128,128]{2,1,0:T(8,128)S(1)} %slice_bitcast_fusion), channel_id=1, source_target_pairs={{0,64},{64,128},{128,192},{192,256},{256,320},{320,384},{384,448},... | collective-permute-start | bytes 393224 | tf_op jit(solution)/shard_map/ppermute | solution.py:14
  5.5 12.3 %collective-permute-done.1 = f32[2,128,128]{2,1,0:T(8,128)S(1)} collective-permute-done((f32[2,128,128]{2,1,0:T(8,128)S(1)}, f32[2,128,128]{2,1,0:T(8,128)S(1)}, u32[]{:S(2)}, u32[]{:S(2)}) %collective-permute-start.1) | collective-permute-done | bytes 131104 | tf_op jit(solution)/shard_map/ppermute | solution.py:14
  17.8 1.9 fusion.7
  19.7 0.9 convolution_bitcast_fusion.8
  20.6 1.2 copy.11
  21.8 21.2 %all-to-all-start = ((f32[4,2,128,128]{3,1,0,2:T(2,128)}), f32[4,2,128,128]{3,1,0,2:T(2,128)S(1)}, u32[]{:S(2)}, u32[]{:S(2)}) async-start(f32[4,2,128,128]{3,1,0,2:T(2,128)} %copy.11), calls=%async_computation | async-start | bytes 1048576 | tf_op jit(solution)/shard_map/all_to_all | solution.py:61
  43.0 4.0 collective-permute-start.3
  47.0 2.7 collective-permute-done.3
  49.6 0.8 fusion.5
  50.5 0.9 convolution_bitcast_fusion.5
  51.4 1.2 copy.17
  52.6 48.9 %all-to-all-done = f32[4,2,128,128]{3,1,0,2:T(2,128)S(1)} async-done(((f32[4,2,128,128]{3,1,0,2:T(2,128)}), f32[4,2,128,128]{3,1,0,2:T(2,128)S(1)}, u32[]{:S(2)}, u32[]{:S(2)}) %all-to-all-start) | async-done | bytes 524320 | tf_op jit(solution)/shard_map/all_to_all | solution.py:61
  101.5 11.0 %all-to-all-start.2 = ((f32[4,2,128,128]{3,1,0,2:T(2,128)}), f32[4,2,128,128]{3,1,0,2:T(2,128)S(1)}, u32[]{:S(2)}, u32[]{:S(2)}) async-start(f32[4,2,128,128]{3,1,0,2:T(2,128)} %copy.17), calls=%async_computation.2 | async-start | bytes 1048576 | tf_op jit(solution)/shard_map/all_to_all | solution.py:61
  112.4 4.3 collective-permute-start.5
  116.7 1.9 collective-permute-done.5
  118.7 0.8 fusion.3
  119.5 0.9 convolution_bitcast_fusion.2
  120.4 1.2 copy.23
  121.6 53.5 %all-to-all-done.2 = f32[4,2,128,128]{3,1,0,2:T(2,128)S(1)} async-done(((f32[4,2,128,128]{3,1,0,2:T(2,128)}), f32[4,2,128,128]{3,1,0,2:T(2,128)S(1)}, u32[]{:S(2)}, u32[]{:S(2)}) %all-to-all-start.2) | async-done | bytes 524320 | tf_op jit(solution)/shard_map/all_to_all | solution.py:61
  175.1 7.1 %all-to-all-start.4 = ((f32[4,2,128,128]{3,1,0,2:T(2,128)}), f32[4,2,128,128]{3,1,0,2:T(2,128)S(1)}, u32[]{:S(2)}, u32[]{:S(2)}) async-start(f32[4,2,128,128]{3,1,0,2:T(2,128)} %copy.23), calls=%async_computation.4 | async-start | bytes 1048576 | tf_op jit(solution)/shard_map/all_to_all | solution.py:61
  182.3 0.1 broadcast_add_fusion
  182.3 0.1 divide_multiply_fusion
  182.4 0.2 copy.12
  182.6 0.9 fusion.2
  183.5 0.9 convolution_bitcast_fusion.7
  184.4 1.2 copy.13
  185.6 59.3 %all-to-all-done.4 = f32[4,2,128,128]{3,1,0,2:T(2,128)S(1)} async-done(((f32[4,2,128,128]{3,1,0,2:T(2,128)}), f32[4,2,128,128]{3,1,0,2:T(2,128)S(1)}, u32[]{:S(2)}, u32[]{:S(2)}) %all-to-all-start.4) | async-done | bytes 524320 | tf_op jit(solution)/shard_map/all_to_all | solution.py:61
  244.9 7.3 %all-to-all-start.1 = ((f32[4,128,2,128]{3,2,0,1:T(2,128)}), f32[4,128,2,128]{3,2,0,1:T(2,128)S(1)}, u32[]{:S(2)}, u32[]{:S(2)}) async-start(f32[4,128,2,128]{3,2,0,1:T(2,128)} %copy.13), calls=%async_computation.1 | async-start | bytes 1048576 | tf_op jit(solution)/shard_map/all_to_all | solution.py:67
  252.2 0.2 copy.18
  252.4 0.9 fusion.1
  253.3 0.9 convolution_bitcast_fusion.4
  254.1 1.2 copy.19
  255.3 59.5 %all-to-all-done.1 = f32[4,128,2,128]{3,2,0,1:T(2,128)S(1)} async-done(((f32[4,128,2,128]{3,2,0,1:T(2,128)}), f32[4,128,2,128]{3,2,0,1:T(2,128)S(1)}, u32[]{:S(2)}, u32[]{:S(2)}) %all-to-all-start.1) | async-done | bytes 524320 | tf_op jit(solution)/shard_map/all_to_all | solution.py:67
  314.9 7.1 %all-to-all-start.3 = ((f32[4,128,2,128]{3,2,0,1:T(2,128)}), f32[4,128,2,128]{3,2,0,1:T(2,128)S(1)}, u32[]{:S(2)}, u32[]{:S(2)}) async-start(f32[4,128,2,128]{3,2,0,1:T(2,128)} %copy.19), calls=%async_computation.3 | async-start | bytes 1048576 | tf_op jit(solution)/shard_map/all_to_all | solution.py:67
  322.0 0.2 copy.24
  322.2 0.9 fusion
  323.0 0.9 convolution_bitcast_fusion.1
  323.9 1.2 copy.25
  325.1 59.5 %all-to-all-done.3 = f32[4,128,2,128]{3,2,0,1:T(2,128)S(1)} async-done(((f32[4,128,2,128]{3,2,0,1:T(2,128)}), f32[4,128,2,128]{3,2,0,1:T(2,128)S(1)}, u32[]{:S(2)}, u32[]{:S(2)}) %all-to-all-start.3) | async-done | bytes 524320 | tf_op jit(solution)/shard_map/all_to_all | solution.py:67
  384.6 7.1 %all-to-all-start.5 = ((f32[4,128,2,128]{3,2,0,1:T(2,128)}), f32[4,128,2,128]{3,2,0,1:T(2,128)S(1)}, u32[]{:S(2)}, u32[]{:S(2)}) async-start(f32[4,128,2,128]{3,2,0,1:T(2,128)} %copy.25), calls=%async_computation.5 | async-start | bytes 1048576 | tf_op jit(solution)/shard_map/all_to_all | solution.py:67
  391.8 0.0 copy-start.2
  391.8 0.6 copy-done.2
  392.4 4.3 collective-permute-start
  396.7 0.7 collective-permute-done
  397.4 4.2 collective-permute-start.2
  401.7 2.1 collective-permute-done.2
  403.7 3.1 collective-permute-start.4
  406.9 0.6 broadcast_multiply_fusion.2
  407.5 0.6 broadcast_multiply_fusion.1
  408.1 2.6 collective-permute-done.4
  410.7 0.6 broadcast_multiply_fusion
  411.4 0.2 copy.14
  411.6 0.8 fusion.21
  412.4 0.2 copy.20
  412.6 0.8 fusion.18
  413.4 0.9 convolution_bitcast_fusion.3
  414.3 40.1 %all-to-all-done.5 = f32[4,128,2,128]{3,2,0,1:T(2,128)S(1)} async-done(((f32[4,128,2,128]{3,2,0,1:T(2,128)}), f32[4,128,2,128]{3,2,0,1:T(2,128)S(1)}, u32[]{:S(2)}, u32[]{:S(2)}) %all-to-all-start.5) | async-done | bytes 524320 | tf_op jit(solution)/shard_map/all_to_all | solution.py:67
  454.4 0.2 copy.26
  454.6 0.8 fusion.15
  455.5 0.0 copy-start.1
  455.5 0.9 convolution_bitcast_fusion
  456.4 0.2 copy-done.1
  456.5 1.8 multiply_subtract_fusion
  (4 shorter events, 0.0 us)
Async XLA Ops:
  0.9 16.9 %collective-permute-start.1 = (f32[2,128,128]{2,1,0:T(8,128)S(1)}, f32[2,128,128]{2,1,0:T(8,128)S(1)}, u32[]{:S(2)}, u32[]{:S(2)}) collective-permute-start(f32[2,128,128]{2,1,0:T(8,128)S(1)} %slice_bitcast_fusion), channel_id=1, source_target_pairs={{0,64},{64,128},{128,192},{192,256},{256,320},{320,384},{384,448},... | collective-permute-start | bytes 393224 | tf_op jit(solution)/shard_map/ppermute | solution.py:14
  21.8 27.9 %copy-start = (f32[4,2,128,128]{3,2,1,0:T(8,128)S(1)}, f32[4,2,128,128]{3,2,1,0:T(8,128)}, u32[]{:S(2)}) copy-start(f32[4,2,128,128]{3,2,1,0:T(8,128)} %param.3) | copy-start | bytes 1572868
  21.8 79.7 %all-to-all-start = ((f32[4,2,128,128]{3,1,0,2:T(2,128)}), f32[4,2,128,128]{3,1,0,2:T(2,128)S(1)}, u32[]{:S(2)}, u32[]{:S(2)}) async-start(f32[4,2,128,128]{3,1,0,2:T(2,128)} %copy.11), calls=%async_computation | async-start | bytes 1048576 | tf_op jit(solution)/shard_map/all_to_all | solution.py:61
  43.0 6.7 %collective-permute-start.3 = (f32[2,128,128]{2,1,0:T(8,128)S(1)}, f32[2,128,128]{2,1,0:T(8,128)S(1)}, u32[]{:S(2)}, u32[]{:S(2)}) collective-permute-start(f32[2,128,128]{2,1,0:T(8,128)S(1)} %collective-permute-done.1), channel_id=1, source_target_pairs={{0,64},{64,128},{128,192},{192,256},{256,320},{320,384},{384,448},... | collective-permute-start | bytes 393224 | tf_op jit(solution)/shard_map/ppermute | solution.py:14
  101.5 73.6 %all-to-all-start.2 = ((f32[4,2,128,128]{3,1,0,2:T(2,128)}), f32[4,2,128,128]{3,1,0,2:T(2,128)S(1)}, u32[]{:S(2)}, u32[]{:S(2)}) async-start(f32[4,2,128,128]{3,1,0,2:T(2,128)} %copy.17), calls=%async_computation.2 | async-start | bytes 1048576 | tf_op jit(solution)/shard_map/all_to_all | solution.py:61
  112.4 6.2 %collective-permute-start.5 = (f32[2,128,128]{2,1,0:T(8,128)S(1)}, f32[2,128,128]{2,1,0:T(8,128)S(1)}, u32[]{:S(2)}, u32[]{:S(2)}) collective-permute-start(f32[2,128,128]{2,1,0:T(8,128)S(1)} %collective-permute-done.3), channel_id=1, source_target_pairs={{0,64},{64,128},{128,192},{192,256},{256,320},{320,384},{384,448},... | collective-permute-start | bytes 393224 | tf_op jit(solution)/shard_map/ppermute | solution.py:14
  175.1 69.8 %all-to-all-start.4 = ((f32[4,2,128,128]{3,1,0,2:T(2,128)}), f32[4,2,128,128]{3,1,0,2:T(2,128)S(1)}, u32[]{:S(2)}, u32[]{:S(2)}) async-start(f32[4,2,128,128]{3,1,0,2:T(2,128)} %copy.23), calls=%async_computation.4 | async-start | bytes 1048576 | tf_op jit(solution)/shard_map/all_to_all | solution.py:61
  244.9 70.0 %all-to-all-start.1 = ((f32[4,128,2,128]{3,2,0,1:T(2,128)}), f32[4,128,2,128]{3,2,0,1:T(2,128)S(1)}, u32[]{:S(2)}, u32[]{:S(2)}) async-start(f32[4,128,2,128]{3,2,0,1:T(2,128)} %copy.13), calls=%async_computation.1 | async-start | bytes 1048576 | tf_op jit(solution)/shard_map/all_to_all | solution.py:67
  314.9 69.8 %all-to-all-start.3 = ((f32[4,128,2,128]{3,2,0,1:T(2,128)}), f32[4,128,2,128]{3,2,0,1:T(2,128)S(1)}, u32[]{:S(2)}, u32[]{:S(2)}) async-start(f32[4,128,2,128]{3,2,0,1:T(2,128)} %copy.19), calls=%async_computation.3 | async-start | bytes 1048576 | tf_op jit(solution)/shard_map/all_to_all | solution.py:67
  384.6 69.8 %all-to-all-start.5 = ((f32[4,128,2,128]{3,2,0,1:T(2,128)}), f32[4,128,2,128]{3,2,0,1:T(2,128)S(1)}, u32[]{:S(2)}, u32[]{:S(2)}) async-start(f32[4,128,2,128]{3,2,0,1:T(2,128)} %copy.25), calls=%async_computation.5 | async-start | bytes 1048576 | tf_op jit(solution)/shard_map/all_to_all | solution.py:67
  391.8 0.7 copy-start.2
  392.4 5.0 %collective-permute-start = (f32[1]{0:T(128)S(1)}, f32[1]{0:T(128)}, u32[]{:S(2)}, u32[]{:S(2)}) collective-permute-start(f32[1]{0:T(128)S(1)} %bitcast.130), channel_id=1, source_target_pairs={{0,64},{64,128},{128,192},{192,256},{256,320},{320,384},{384,448},... | collective-permute-start | bytes 20 | tf_op jit(solution)/shard_map/ppermute | solution.py:14
  397.4 6.3 %collective-permute-start.2 = (f32[1]{0:T(128)}, f32[1]{0:T(128)}, u32[]{:S(2)}, u32[]{:S(2)}) collective-permute-start(f32[1]{0:T(128)} %collective-permute-done), channel_id=1, source_target_pairs={{0,64},{64,128},{128,192},{192,256},{256,320},{320,384},{384,448},... | collective-permute-start | bytes 20 | tf_op jit(solution)/shard_map/ppermute | solution.py:14
  403.7 7.0 %collective-permute-start.4 = (f32[1]{0:T(128)}, f32[1]{0:T(128)}, u32[]{:S(2)}, u32[]{:S(2)}) collective-permute-start(f32[1]{0:T(128)} %collective-permute-done.2), channel_id=1, source_target_pairs={{0,64},{64,128},{128,192},{192,256},{256,320},{320,384},{384,448},... | collective-permute-start | bytes 20 | tf_op jit(solution)/shard_map/ppermute | solution.py:14
  455.5 1.0 copy-start.1
where the time goes:
time: 461 us; the launch traced here: 458 us
  waiting for transfers between devices  343 us (74%)
  starting transfers between devices  85.3 us (19%)
  matrix products  17.3 us (4%)
  local copies, waits for them, and re-layouts  10.1 us (2%)
    all_to_all x3, waiting for transfers between devices, body(): lax.all_to_all(potentials_spectra, 'slab', split_axis=2, concat_axis=1, t...  162 us
    all_to_all x3, waiting for transfers between devices, body(): lax.all_to_all(columns, 'slab', split_axis=1, concat_axis=2, tiled=True)  159 us
    all_to_all x3, starting transfers between devices, body(): lax.all_to_all(potentials_spectra, 'slab', split_axis=2, concat_axis=1, t...  39.2 us
    ppermute x6, starting transfers between devices, shifted(): return lax.ppermute(value, axis, pairs)  24.6 us
    ppermute x6, waiting for transfers between devices, shifted(): return lax.ppermute(value, axis, pairs)  22.3 us
    all_to_all x3, starting transfers between devices, body(): lax.all_to_all(columns, 'slab', split_axis=1, concat_axis=2, tiled=True)  21.5 us
  transfers between devices with their start and end apart: 12, of which 12 were waited for; matrix products, arithmetic and copies ran while one was open for 4% of the time, Pallas kernels for 0%

commit v1 on v0

v1 whole, which is shorter than its diff:
```python
import functools
import math

import jax
import jax.numpy as jnp
import ml_dtypes
import numpy as np
from jax import lax
from jax.experimental import pallas as pl
from jax.experimental.pallas import tpu as pltpu
from jax.sharding import PartitionSpec as P

MESH = pl.DeviceIdType.MESH
F32 = jnp.float32
BF16 = jnp.bfloat16
SUB = 8

(
    IN_PV, IN_PR0, IN_PR1, IN_OCC, IN_CV, IN_R, IN_VD, IN_VF, IN_T, IN_U, IN_Q, IN_RET, N_IN
) = (0, 1, 2, 3, 4, 5, 6, 9, 12, 15, 18, 19, 20)


def hartley(extent):
    index = np.arange(extent)
    angle = (index[:, None] * index[None, :] % extent) * (2.0 * math.pi / extent)
    full = np.cos(angle) + np.sin(angle)
    high = full.astype(ml_dtypes.bfloat16)
    low = (full - high.astype(np.float64)).astype(ml_dtypes.bfloat16)
    return high, low


def split(value):
    high = value.astype(BF16)
    low = (value - high.astype(F32)).astype(BF16)
    return high, low


def rows_times(value, matrix):
    n = value.shape[1]
    both = jnp.concatenate(split(value), axis=1)
    out = jnp.dot(both, matrix, preferred_element_type=F32)
    return out[:, :n] + out[:, n:]


def times_columns(matrix, value):
    n = value.shape[0]
    both = jnp.concatenate(split(value), axis=0)
    out = jnp.dot(matrix, both, preferred_element_type=F32)
    return out[:n] + out[n:]


def kernel(
    bands, extent,
    orb, occ, acc, right_mat, left_mat, out,
    pv, pr0, pr1, occ_own, occ_all, cv, res, vis, mid, fwd, tin, tout, back, done, ret_z, ret,
    send_sem, in_sem,
):
    nz, nw = 2 * bands, bands
    b, s = lax.axis_index("band"), lax.axis_index("slab")
    z, yh, g = s // 2, s % 2, b % 2
    w = (b // 2) * 2 + yh
    place = 2 * w + g

    def device(tw, tg, tz):
        return {"band": (tw // 2) * 2 + tg, "slab": 2 * tz + tw % 2}

    def push(src, dst, sem, target):
        pltpu.make_async_remote_copy(
            src_ref=src, dst_ref=dst, send_sem=send_sem.at[sem], recv_sem=in_sem.at[sem],
            device_id=target, device_id_type=MESH,
        ).start()

    def keep(src, dst, sem):
        pltpu.make_async_copy(src, dst, in_sem.at[sem]).start()

    def arrived(ref, sem):
        pltpu.make_async_copy(ref, ref, in_sem.at[sem]).wait()

    def sent(ref, sem):
        pltpu.make_async_copy(ref, ref, send_sem.at[sem]).wait()

    def loop(low, high, fn):
        def step(i, carry):
            fn(i)
            return carry
        lax.fori_loop(low, high, step, 0)

    occ_own[...] = jnp.full(occ_own.shape, occ[0], F32)

    barrier = pltpu.get_barrier_semaphore()

    def greet(target):
        pl.semaphore_signal(barrier, inc=1, device_id=target, device_id_type=MESH)

    def greet_plane(d):
        t = (place + d) % (2 * nw)
        greet(device(t // 2, t % 2, z))

    loop(1, nz, lambda d: greet(device(w, g, (z + d) % nz)))
    loop(1, 2 * nw, greet_plane)

    @pl.when(g == 0)
    def _():
        greet(device(w, 1, (z + 3) % nz))

    pl.semaphore_wait(barrier, 2 * nw - 1 + nz - 1 + g)

    mine = 2 * b + yh

    def visitors_out(d):
        t = (place + d) % (2 * nw)
        push(orb.at[0, t % 2, t // 2], pv.at[mine], IN_PV, device(t // 2, t % 2, z))

    def residents_out(d):
        t = (place + d) % (2 * nw)
        tw, tg = t // 2, t % 2
        push(orb.at[2 + tg, :, tw], pr0.at[mine], IN_PR0, device(tw, tg, z))

    def seconds_out(d):
        tw = (w + d) % nw
        push(orb.at[1, :, tw], pr1.at[mine], IN_PR1, device(tw, 1, z))

    def weights_out(d):
        t = (place + d) % (2 * nw)
        tw, tg = t // 2, t % 2

        @pl.when(tw % 2 == yh)
        def _():
            push(occ_own, occ_all.at[b], IN_OCC, device(tw, tg, z))

    loop(1, 2 * nw, visitors_out)
    keep(orb.at[0, g, w], pv.at[mine], IN_PV)
    loop(1, 2 * nw, residents_out)
    keep(orb.at[2 + g, :, w], pr0.at[mine], IN_PR0)
    loop(1, nw, seconds_out)

    @pl.when(g == 0)
    def _():
        push(orb.at[1, :, w], pr1.at[mine], IN_PR1, device(w, 1, z))

    @pl.when(g == 1)
    def _():
        keep(orb.at[1, :, w], pr1.at[mine], IN_PR1)

    loop(1, 2 * nw, weights_out)
    keep(occ_own, occ_all.at[b], IN_OCC)

    half = bands // 2

    def signed(m):
        reach = half - (m + 1) // 2
        return jnp.where(m % 2 == 0, reach, -reach)

    def centre_out(m):
        tz = (z // 2 * 2 + 2 * signed(m) + nz) % nz
        owner = (tz // 2 - 2 + bands) % bands
        src, dst = pv.at[pl.ds(2 * owner, 2)], cv.at[pl.ds(2 * z, 2)]

        @pl.when(tz == z)
        def _():
            keep(src, dst, IN_CV)

        @pl.when(tz != z)
        def _():
            push(src, dst, IN_CV, device(w, g, tz))

    def home_out(m, stage, odd):
        tz = (z // 2 * 2 + 2 * signed(m) + odd + nz) % nz
        owner = tz // 2
        src, dst = stage.at[pl.ds(2 * owner, 2)], res.at[pl.ds(2 * z, 2)]

        @pl.when(tz == z)
        def _():
            keep(src, dst, IN_R)

        @pl.when(tz != z)
        def _():
            push(src, dst, IN_R, device(w, g, tz))

    arrived(pv, IN_PV)
    loop(0, bands, centre_out)
    arrived(pr0, IN_PR0)
    loop(0, bands, lambda m: home_out(m, pr0, 0))

    @pl.when(g == 1)
    def _():
        arrived(pr1, IN_PR1)
        loop(0, bands, lambda m: home_out(m, pr1, 1))

    @pl.when(z % 2 == 0)
    def _():
        arrived(cv, IN_CV)
        keep(cv, vis.at[1, :, g], IN_VD + 1)
        for d, h in ((1, 1), (-1, 0), (-2, 0), (2, 2), (3, 2)):
            push(cv, vis.at[h, :, g], IN_VD + h, device(w, g, (z + d + nz) % nz))
        push(cv, res.at[:, g], IN_R, device(w, 0, (z - 3 + nz) % nz))

    order = (1, 0, 2)

    def share(h):
        half_vis = vis.at[h, :, g]
        arrived(half_vis, IN_VD + h)
        push(half_vis, half_vis, IN_VF + h, device(w, 1 - g, z))

    def transform_x(src, dst):
        for y in range(0, SUB, 2):
            two = jnp.concatenate(
                [src[pl.ds(y + k, extent, stride=SUB), :] for k in range(2)], axis=1
            )
            two = times_columns(left_mat[...], two)
            for k in range(2):
                dst[pl.ds(y + k, extent, stride=SUB), :] = two[:, k * extent:(k + 1) * extent]

    rows = extent * SUB
    slab_rows = SUB * SUB
    for h in order:
        share(h)
    arrived(res, IN_R)
    for h in order:
        arrived(vis.at[h, :, 1 - g], IN_VF + h)
        pair = (res[...] * vis[h]).reshape(rows, extent)
        mid[...] = rows_times(pair, right_mat[...])
        transform_x(mid, fwd.at[h])

        def fwd_out(d, h=h):
            tw = (w + d) % nw
            push(fwd.at[h, pl.ds(slab_rows * tw, slab_rows)], tin.at[h, w], IN_T + h, device(tw, g, z))

        loop(1, nw, fwd_out)
        keep(fwd.at[h, pl.ds(slab_rows * w, slab_rows)], tin.at[h, w], IN_T + h)

    def wave(index):
        near = jnp.where(index < extent // 2, index, index - extent)
        return near.astype(F32) * (2.0 * math.pi / extent)

    shape = (extent, extent)
    square = (
        wave(lax.broadcasted_iota(jnp.int32, shape, 0)) ** 2
        + wave(lax.broadcasted_iota(jnp.int32, shape, 1)) ** 2
    )

    def screening(a):
        index = SUB * w + a
        return (4.0 * math.pi / float(extent**3)) / (square + wave(index) ** 2 + 0.01)

    for h in order:
        arrived(tin.at[h], IN_T + h)
        for a in range(0, SUB, 2):
            two = jnp.concatenate(
                [tin[h, :, SUB * (a + k):SUB * (a + k + 1), :].reshape(shape) for k in range(2)],
                axis=1,
            )
            two = times_columns(left_mat[...], two)
            two = two * jnp.concatenate([screening(a), screening(a + 1)], axis=1)
            two = times_columns(left_mat[...], two)
            for k in range(2):
                tout[h, :, SUB * (a + k):SUB * (a + k + 1), :] = two[
                    :, k * extent:(k + 1) * extent
                ].reshape(nw, SUB, extent)

        def back_out(d, h=h):
            tw = (w + d) % nw
            push(tout.at[h, tw], back.at[h, pl.ds(slab_rows * w, slab_rows)], IN_U + h, device(tw, g, z))

        loop(1, nw, back_out)
        keep(tout.at[h, w], back.at[h, pl.ds(slab_rows * w, slab_rows)], IN_U + h)

    arrived(occ_all, IN_OCC)
    for h in order:
        arrived(back.at[h], IN_U + h)
        transform_x(back.at[h], mid)
        potential = rows_times(mid[...], right_mat[...]).reshape(extent // 2, 2, SUB, extent)
        owner = (z // 2 - (h + 1) + bands) % bands
        term = vis[h] * potential * occ_all[owner][None, None]
        term = term.reshape(done.shape)
        if h == order[0]:
            done[...] = term
        else:
            done[...] += term

    def slabs_out(m):
        reach = nz // 2 - m // 2
        tz = (z + jnp.where(m % 2 == 1, reach, nz - reach)) % nz
        push(done.at[tz], ret_z.at[z // 2, z % 2], IN_Q, device(w, g, tz))

    loop(1, nz, slabs_out)
    keep(done.at[z], ret_z.at[z // 2, z % 2], IN_Q)
    arrived(ret_z, IN_Q)

    def owners_out(d):
        t = (place + d) % (2 * nw)
        tw, tg = t // 2, t % 2
        owner = (tw // 2) * 2 + tg
        push(ret_z.at[owner, :, tw % 2], ret.at[:, g, :, w], IN_RET, device(tw, tg, z))

    loop(1, 2 * nw, owners_out)
    keep(ret_z.at[b, :, yh], ret.at[:, g, :, w], IN_RET)
    arrived(ret, IN_RET)
    for first in range(2):
        for core in range(2):
            j = 2 * (1 - first) + core
            out[j] = acc[j] - ret[first, core]

    sent(pv.at[pl.ds(1, 2 * nw - 1)], IN_PV)
    sent(pr0.at[pl.ds(1, 2 * nw - 1)], IN_PR0)
    sent(pr1.at[pl.ds(0, nw - 1)], IN_PR1)

    @pl.when(g == 0)
    def _():
        sent(pr1.at[0], IN_PR1)

    sent(occ_all.at[pl.ds(0, nw - 1)], IN_OCC)
    sent(cv.at[pl.ds(0, 2 * bands - 2)], IN_CV)
    sent(res.at[pl.ds(0, 2 * bands - 2)], IN_R)

    @pl.when(z % 2 == 1)
    def _():
        sent(cv.at[pl.ds(0, 2)], IN_CV)
        sent(res.at[pl.ds(0, 2)], IN_R)

    @pl.when(g == 1)
    def _():
        sent(res.at[pl.ds(0, 2 * bands - 2)], IN_R)

    @pl.when(jnp.logical_and(g == 1, z % 2 == 0))
    def _():
        sent(res.at[pl.ds(0, 2)], IN_R)

    @pl.when(z % 2 == 0)
    def _():
        sent(res.at[:, g], IN_R)
        for h in (1, 0, 0, 2, 2):
            sent(cv, IN_VD + h)

    for h in order:
        sent(vis.at[h, :, g], IN_VF + h)
        sent(tin.at[h, pl.ds(0, nw - 1)], IN_T + h)
        sent(tout.at[h, pl.ds(0, nw - 1)], IN_U + h)
    sent(done.at[pl.ds(0, nz - 1)], IN_Q)
    sent(done.at[pl.ds(0, 2 * nw - 1)], IN_RET)


def body(orbitals, occupations, accumulated):
    extent = orbitals.shape[2]
    bands = lax.axis_size("band")
    nz, nw = 2 * bands, bands
    high, low = hartley(extent)
    right_mat = jnp.asarray(np.block([[high, low], [high, low]]))
    left_mat = jnp.asarray(np.block([[high, high], [low, low]]))
    tiled = (orbitals.shape[0], orbitals.shape[1], nw, SUB, extent)
    rows = extent * SUB
    tile = (SUB, extent)
    vmem = pl.BlockSpec(memory_space=pltpu.VMEM)
    scratch = [
        (2 * bands, *tile),
        (2 * bands, 2, *tile),
        (2 * bands, 2, *tile),
        tile,
        (bands, *tile),
        (2 * nz, *tile),
        (2 * nz, 2, *tile),
        (3, 2 * nz, 2, *tile),
        (rows, extent),
        (3, rows, extent),
        (3, nw, SUB * SUB, extent),
        (3, nw, SUB * SUB, extent),
        (3, rows, extent),
        (nz, 2, 2, *tile),
        (bands, 2, 2, 2, *tile),
        (2, 2, 2, nw, *tile),
    ]
    result = pl.pallas_call(
        functools.partial(kernel, bands, extent),
        out_shape=jax.ShapeDtypeStruct(tiled, F32),
        in_specs=[vmem, pl.BlockSpec(memory_space=pltpu.SMEM), vmem, vmem, vmem],
        out_specs=vmem,
        scratch_shapes=[pltpu.VMEM(shape, F32) for shape in scratch]
        + [pltpu.SemaphoreType.DMA((N_IN,)), pltpu.SemaphoreType.DMA((N_IN,))],
        compiler_params=pltpu.CompilerParams(
            collective_id=0, has_side_effects=True, vmem_limit_bytes=40 * 2**20
        ),
    )(orbitals.reshape(tiled), occupations, accumulated.reshape(tiled), right_mat, left_mat)
    return result.reshape(orbitals.shape)


def solution(mesh):
    in_specs = (P("band", "slab", None, None), P("band"), P("band", "slab", None, None))
    out_specs = P("band", "slab", None, None)
    return jax.shard_map(body, mesh=mesh, in_specs=in_specs, out_specs=out_specs, check_vma=False)
```

time: 461 us -> 200 us (0.43)
  waiting for transfers between devices: 343 us -> 0 us
  Pallas kernels: 0 us -> 195 us
  starting transfers between devices: 85.3 us -> 0 us
  matrix products: 17.3 us -> 0 us
  local copies, waits for them, and re-layouts: 10.1 us -> 5.34 us
    all_to_all x6 -> x0, waiting for transfers between devices: 321 us -> none  [the longest x3 162 us: body(): lax.all_to_all(potentials_spectra, 'slab', split_axis=2, concat_axis=1, t...]
    pallas_call x0 -> x1, Pallas kernels: none -> 195 us  [body(): pl.pallas_call(functools.partial(kernel, bands, extent), out_shape=jax.Sh...]
    all_to_all x6 -> x0, starting transfers between devices: 60.7 us -> none  [the longest x3 39.2 us: body(): lax.all_to_all(potentials_spectra, 'slab', split_axis=2, concat_axis=1, t...]
    ppermute x6 -> x0, starting transfers between devices: 24.6 us -> none  [shifted(): return lax.ppermute(value, axis, pairs)]
    ppermute x6 -> x0, waiting for transfers between devices: 22.3 us -> none  [shifted(): return lax.ppermute(value, axis, pairs)]
    dot_general x18 -> x0, matrix products: 17.3 us -> none  [the longest x6 6.08 us: transform_inner(): return jnp.einsum('pxyc,yb->pxbc', spectra, matrix, precision=highest)]
    transpose x6 -> x0, local copies, waits for them, and re-layouts: 7.19 us -> none  [the longest x3 3.6 us: body(): columns = jnp.einsum('pabc,ax->pxbc', columns, matrix, precision=highest)]
  transfers between devices with their start and end apart: 12 -> 0, of which waited for: 12 -> 0; matrix products, arithmetic and copies ran while one was open for 4% -> 0% of each run, Pallas kernels for 0% -> 0%
where the time goes in v1:
time: 200 us
  Pallas kernels  195 us (98%)
  local copies, waits for them, and re-layouts  5.34 us (3%)
    pallas_call x1, Pallas kernels, body(): pl.pallas_call(functools.partial(kernel, bands, extent), out_shape=jax.Sh...  195 us
    unnamed x11, local copies, waits for them, and re-layouts  5.34 us

profile of v1, /device:TPU:1, one launch (start us, length us, event | category | flops | bytes accessed | tf_op | source)
XLA Modules:
  0.0 200.0 jit_solution(4901599751882482510)
XLA Ops:
  0.0 0.0 copy-start.4
  0.0 0.7 copy-done.4
  0.7 0.0 copy-start
  0.7 1.0 copy-done
  1.7 0.0 copy-start.1
  1.7 1.0 copy-done.1
  2.7 0.0 copy-start.2
  2.7 0.9 copy-done.2
  3.6 0.0 copy-start.3
  3.6 0.9 copy-done.3
  4.5 194.6 %shard_map.55 = f32[4,2,16,8,128]{4,3,2,1,0:T(8,128)S(1)} custom-call(f32[4,2,16,8,128]{4,3,2,1,0:T(8,128)S(1)} %bitcast.4, f32[4]{0:T(128)S(1)} %copy-done.4, f32[4,2,16,8,128]{4,3,2,1,0:T(8,128)S(1)} %bitcast.5, bf16[256,256]{1,0:T(8,128)(2,1)S(1)} %copy-done.3, bf16[256,256]{1,0:T(8,128)(2,1)S(1)} %copy-done.2), custom_call_target="tpu_custom_call" | custom-call | tf_op jit(solution)/shard_map/pallas_call | solution.py:372
  199.2 0.8 copy.7
Async XLA Ops:
  0.0 0.7 copy-start.4
  0.7 1.0 copy-start
  1.7 1.0 copy-start.1
  2.7 0.9 copy-start.2
  3.6 0.9 copy-start.3

commit v2 on v1

--- a/solution.py
+++ b/solution.py
@@ -15,9 +15,12 @@
 BF16 = jnp.bfloat16
 SUB = 8
 
-(
-    IN_PV, IN_PR0, IN_PR1, IN_OCC, IN_CV, IN_R, IN_VD, IN_VF, IN_T, IN_U, IN_Q, IN_RET, N_IN
-) = (0, 1, 2, 3, 4, 5, 6, 9, 12, 15, 18, 19, 20)
+CHUNKS = 4
+
+IN_PV, IN_PR0, IN_PR1, IN_OCC, IN_CV, IN_R = range(6)
+IN_VF, IN_T, IN_U, IN_RET, IN_Q, IN_ACC, IN_MAT, OUT_CHAIN = 6, 9, 12, 15, 17, 18, 19, 20
+IN_VD = 21
+N_SEM = IN_VD + 3 * CHUNKS
 
 
 def hartley(extent):
@@ -51,9 +54,9 @@
 
 def kernel(
     bands, extent,
-    orb, occ, acc, right_mat, left_mat, out,
-    pv, pr0, pr1, occ_own, occ_all, cv, res, vis, mid, fwd, tin, tout, back, done, ret_z, ret,
-    send_sem, in_sem,
+    orb, occ, acc_hbm, right_hbm, left_hbm, out,
+    acc, right_mat, left_mat, pv, pr0, pr1, occ_own, occ_all, cv, res, vis, mid, fwd, tin, tout, back, done, ret_z, ret,
+    send_sem, in_sem, turn,
 ):
     nz, nw = 2 * bands, bands
     b, s = lax.axis_index("band"), lax.axis_index("slab")
@@ -64,9 +67,10 @@
     def device(tw, tg, tz):
         return {"band": (tw // 2) * 2 + tg, "slab": 2 * tz + tw % 2}
 
-    def push(src, dst, sem, target):
+    def push(src, dst, sem, target, leave=None):
         pltpu.make_async_remote_copy(
-            src_ref=src, dst_ref=dst, send_sem=send_sem.at[sem], recv_sem=in_sem.at[sem],
+            src_ref=src, dst_ref=dst, recv_sem=in_sem.at[sem],
+            send_sem=send_sem.at[sem if leave is None else leave],
             device_id=target, device_id_type=MESH,
         ).start()
 
@@ -85,6 +89,9 @@
             return carry
         lax.fori_loop(low, high, step, 0)
 
+    keep(acc_hbm, acc, IN_ACC)
+    keep(right_hbm, right_mat, IN_MAT)
+    keep(left_hbm, left_mat, IN_MAT)
     occ_own[...] = jnp.full(occ_own.shape, occ[0], F32)
 
     barrier = pltpu.get_barrier_semaphore()
@@ -101,7 +108,7 @@
 
     @pl.when(g == 0)
     def _():
-        greet(device(w, 1, (z + 3) % nz))
+        greet(device(w, 1, (z + 1) % nz))
 
     pl.semaphore_wait(barrier, 2 * nw - 1 + nz - 1 + g)
 
@@ -132,18 +139,6 @@
     keep(orb.at[0, g, w], pv.at[mine], IN_PV)
     loop(1, 2 * nw, residents_out)
     keep(orb.at[2 + g, :, w], pr0.at[mine], IN_PR0)
-    loop(1, nw, seconds_out)
-
-    @pl.when(g == 0)
-    def _():
-        push(orb.at[1, :, w], pr1.at[mine], IN_PR1, device(w, 1, z))
-
-    @pl.when(g == 1)
-    def _():
-        keep(orb.at[1, :, w], pr1.at[mine], IN_PR1)
-
-    loop(1, 2 * nw, weights_out)
-    keep(occ_own, occ_all.at[b], IN_OCC)
 
     half = bands // 2
 
@@ -179,27 +174,84 @@
 
     arrived(pv, IN_PV)
     loop(0, bands, centre_out)
-    arrived(pr0, IN_PR0)
-    loop(0, bands, lambda m: home_out(m, pr0, 0))
+
+    loop(1, nw, seconds_out)
+
+    @pl.when(g == 0)
+    def _():
+        push(orb.at[1, :, w], pr1.at[mine], IN_PR1, device(w, 1, z))
 
     @pl.when(g == 1)
     def _():
-        arrived(pr1, IN_PR1)
-        loop(0, bands, lambda m: home_out(m, pr1, 1))
-
-    @pl.when(z % 2 == 0)
+        keep(orb.at[1, :, w], pr1.at[mine], IN_PR1)
+
+    loop(1, 2 * nw, weights_out)
+    keep(occ_own, occ_all.at[b], IN_OCC)
+
+    even = z % 2 == 0
+    above, below = device(w, g, (z + 1) % nz), device(w, g, (z - 1 + nz) % nz)
+    piece = 2 * nz // CHUNKS
+
+    def visitor(h, k):
+        return vis.at[h, pl.ds(piece * k, piece), g]
+
+    def pass_on(src, h, k, target):
+        push(src, visitor(h, k), IN_VD + CHUNKS * h + k, target, OUT_CHAIN)
+
+    def came(h, k):
+        arrived(visitor(h, k), IN_VD + CHUNKS * h + k)
+
+    sent(pv.at[pl.ds(0, 2 * bands - 2)], IN_CV)
+
+    @pl.when(even)
     def _():
         arrived(cv, IN_CV)
-        keep(cv, vis.at[1, :, g], IN_VD + 1)
-        for d, h in ((1, 1), (-1, 0), (-2, 0), (2, 2), (3, 2)):
-            push(cv, vis.at[h, :, g], IN_VD + h, device(w, g, (z + d + nz) % nz))
-        push(cv, res.at[:, g], IN_R, device(w, 0, (z - 3 + nz) % nz))
+        for k in range(CHUNKS):
+            part = cv.at[pl.ds(piece * k, piece)]
+            pass_on(part, 1, k, above)
+            pass_on(part, 0, k, below)
+        for k in range(CHUNKS):
+            keep(cv.at[pl.ds(piece * k, piece)], visitor(1, k), IN_VD + CHUNKS + k)
+
+    @pl.when(jnp.logical_not(even))
+    def _():
+        sent(pv.at[pl.ds(0, 2)], IN_CV)
+
+    @pl.when(even)
+    def _():
+        for k in range(CHUNKS):
+            came(0, k)
+            push(
+                visitor(0, k), res.at[pl.ds(piece * k, piece), g], IN_R,
+                device(w, 0, (z - 1 + nz) % nz), OUT_CHAIN,
+            )
+            came(2, k)
+            pass_on(visitor(2, k), 2, k, above)
+        for k in range(CHUNKS):
+            came(1, k)
+
+    @pl.when(jnp.logical_not(even))
+    def _():
+        for k in range(CHUNKS):
+            came(0, k)
+            pass_on(visitor(0, k), 0, k, below)
+            came(1, k)
+            pass_on(visitor(1, k), 2, k, above)
+
+    @pl.when(g == 0)
+    def _():
+        arrived(pr0, IN_PR0)
+        loop(0, bands, lambda m: home_out(m, pr0, 0))
+
+    @pl.when(jnp.logical_not(even))
+    def _():
+        for k in range(CHUNKS):
+            came(2, k)
 
     order = (1, 0, 2)
 
     def share(h):
         half_vis = vis.at[h, :, g]
-        arrived(half_vis, IN_VD + h)
         push(half_vis, half_vis, IN_VF + h, device(w, 1 - g, z))
 
     def transform_x(src, dst):
@@ -215,6 +267,31 @@
     slab_rows = SUB * SUB
     for h in order:
         share(h)
+
+    @pl.when(g == 0)
+    def _():
+        sent(res.at[pl.ds(0, 2 * bands - 2)], IN_R)
+
+        @pl.when(jnp.logical_not(even))
+        def _():
+            sent(res.at[pl.ds(0, 2)], IN_R)
+
+        pl.semaphore_signal(turn, inc=1, device_id=device(w, 1, z), device_id_type=MESH)
+
+    @pl.when(g == 1)
+    def _():
+        arrived(pr0, IN_PR0)
+        arrived(pr1, IN_PR1)
+        pl.semaphore_wait(turn, 1)
+
+        def both(m):
+            home_out(m, pr0, 0)
+            home_out(m, pr1, 1)
+
+        loop(0, bands, both)
+
+    arrived(right_mat, IN_MAT)
+    arrived(left_mat, IN_MAT)
     arrived(res, IN_R)
     for h in order:
         arrived(vis.at[h, :, 1 - g], IN_VF + h)
@@ -291,13 +368,14 @@
         t = (place + d) % (2 * nw)
         tw, tg = t // 2, t % 2
         owner = (tw // 2) * 2 + tg
-        push(ret_z.at[owner, :, tw % 2], ret.at[:, g, :, w], IN_RET, device(tw, tg, z))
+        push(ret_z.at[owner, :, tw % 2], ret.at[:, g, :, w], IN_RET + g, device(tw, tg, z), IN_RET)
 
     loop(1, 2 * nw, owners_out)
-    keep(ret_z.at[b, :, yh], ret.at[:, g, :, w], IN_RET)
-    arrived(ret, IN_RET)
-    for first in range(2):
-        for core in range(2):
+    keep(ret_z.at[b, :, yh], ret.at[:, g, :, w], IN_RET + g)
+    arrived(acc, IN_ACC)
+    for core in range(2):
+        arrived(ret.at[:, core], IN_RET + core)
+        for first in range(2):
             j = 2 * (1 - first) + core
             out[j] = acc[j] - ret[first, core]
 
@@ -310,27 +388,19 @@
         sent(pr1.at[0], IN_PR1)
 
     sent(occ_all.at[pl.ds(0, nw - 1)], IN_OCC)
-    sent(cv.at[pl.ds(0, 2 * bands - 2)], IN_CV)
-    sent(res.at[pl.ds(0, 2 * bands - 2)], IN_R)
-
-    @pl.when(z % 2 == 1)
-    def _():
-        sent(cv.at[pl.ds(0, 2)], IN_CV)
-        sent(res.at[pl.ds(0, 2)], IN_R)
 
     @pl.when(g == 1)
     def _():
-        sent(res.at[pl.ds(0, 2 * bands - 2)], IN_R)
-
-    @pl.when(jnp.logical_and(g == 1, z % 2 == 0))
-    def _():
-        sent(res.at[pl.ds(0, 2)], IN_R)
-
-    @pl.when(z % 2 == 0)
-    def _():
-        sent(res.at[:, g], IN_R)
-        for h in (1, 0, 0, 2, 2):
-            sent(cv, IN_VD + h)
+        sent(res.at[pl.ds(0, 2 * bands - 1)], IN_R)
+        sent(res.at[pl.ds(0, 2 * bands - 1)], IN_R)
+
+    sent(cv, OUT_CHAIN)
+    sent(cv, OUT_CHAIN)
+
+    @pl.when(even)
+    def _():
+        sent(cv, OUT_CHAIN)
+        sent(cv, OUT_CHAIN)
 
     for h in order:
         sent(vis.at[h, :, g], IN_VF + h)
@@ -351,6 +421,7 @@
     rows = extent * SUB
     tile = (SUB, extent)
     vmem = pl.BlockSpec(memory_space=pltpu.VMEM)
+    hbm = pl.BlockSpec(memory_space=pltpu.HBM)
     scratch = [
         (2 * bands, *tile),
         (2 * bands, 2, *tile),
@@ -372,12 +443,15 @@
     result = pl.pallas_call(
         functools.partial(kernel, bands, extent),
         out_shape=jax.ShapeDtypeStruct(tiled, F32),
-        in_specs=[vmem, pl.BlockSpec(memory_space=pltpu.SMEM), vmem, vmem, vmem],
+        in_specs=[hbm, pl.BlockSpec(memory_space=pltpu.SMEM), hbm, hbm, hbm],
         out_specs=vmem,
-        scratch_shapes=[pltpu.VMEM(shape, F32) for shape in scratch]
-        + [pltpu.SemaphoreType.DMA((N_IN,)), pltpu.SemaphoreType.DMA((N_IN,))],
+        scratch_shapes=[pltpu.VMEM(tiled, F32)]
+        + [pltpu.VMEM((2 * extent, 2 * extent), BF16)] * 2
+        + [pltpu.VMEM(shape, F32) for shape in scratch]
+        + [pltpu.SemaphoreType.DMA((N_SEM,))] * 2
+        + [pltpu.SemaphoreType.REGULAR],
         compiler_params=pltpu.CompilerParams(
-            collective_id=0, has_side_effects=True, vmem_limit_bytes=40 * 2**20
+            collective_id=0, has_side_effects=True, vmem_limit_bytes=60 * 2**20
         ),
     )(orbitals.reshape(tiled), occupations, accumulated.reshape(tiled), right_mat, left_mat)
     return result.reshape(orbitals.shape)

time: 200 us -> 168 us (0.84)
  Pallas kernels: 195 us -> 166 us
  local copies, waits for them, and re-layouts: 5.34 us -> 1.87 us
    pallas_call x1, Pallas kernels: 195 us -> 166 us  [body(): pl.pallas_call(functools.partial(kernel, bands, extent), out_shape=jax.Sh...]
    unnamed x11 -> x1, local copies, waits for them, and re-layouts: 5.34 us -> 1.87 us
where the time goes in v2:
time: 168 us
  Pallas kernels  166 us (99%)
  local copies, waits for them, and re-layouts  1.87 us (1%)
    pallas_call x1, Pallas kernels, body(): pl.pallas_call(functools.partial(kernel, bands, extent), out_shape=jax.Sh...  166 us

profile of v2, /device:TPU:1, one launch (start us, length us, event | category | flops | bytes accessed | tf_op | source)
XLA Modules:
  0.0 167.6 jit_solution(5023297598522766709)
XLA Ops:
  0.0 165.7 %shard_map.55 = f32[4,2,16,8,128]{4,3,2,1,0:T(8,128)} custom-call(f32[4,2,16,8,128]{4,3,2,1,0:T(8,128)} %bitcast.4, f32[4]{0:T(128)} %occ.1, f32[4,2,16,8,128]{4,3,2,1,0:T(8,128)} %bitcast.5, bf16[256,256]{1,0:T(8,128)(2,1)} %constant.4.clone.right_hbm, bf16[256,256]{1,0:T(8,128)(2,1)} %constant.5.clone.left_hbm), custom_call_target="tpu_custom_call" | custom-call | tf_op jit(solution)/shard_map/pallas_call | solution.py:443
  165.7 1.9 %copy.7 = f32[4,2,128,128]{3,2,1,0:T(8,128)} copy(f32[4,2,128,128]{3,2,1,0:T(8,128)} %bitcast.3) | data formatting | bytes 1048576

commit v3 on v2

--- a/solution.py
+++ b/solution.py
@@ -18,9 +18,9 @@
 CHUNKS = 4
 
 IN_PV, IN_PR0, IN_PR1, IN_OCC, IN_CV, IN_R = range(6)
-IN_VF, IN_T, IN_U, IN_RET, IN_Q, IN_ACC, IN_MAT, OUT_CHAIN = 6, 9, 12, 15, 17, 18, 19, 20
+IN_VF, IN_T, IN_U, IN_RET, OUT_Q, IN_ACC, IN_MAT, OUT_CHAIN = 6, 9, 12, 15, 17, 18, 19, 20
 IN_VD = 21
-N_SEM = IN_VD + 3 * CHUNKS
+IN_Q = IN_VD + 3 * CHUNKS
 
 
 def hartley(extent):
@@ -103,7 +103,11 @@
         t = (place + d) % (2 * nw)
         greet(device(t // 2, t % 2, z))
 
-    loop(1, nz, lambda d: greet(device(w, g, (z + d) % nz)))
+    def far_first(m):
+        reach = nz // 2 - m // 2
+        return (z + jnp.where(m % 2 == 1, reach, nz - reach)) % nz
+
+    loop(1, nz, lambda m: greet(device(w, g, far_first(m))))
     loop(1, 2 * nw, greet_plane)
 
     @pl.when(g == 0)
@@ -216,6 +220,11 @@
     @pl.when(jnp.logical_not(even))
     def _():
         sent(pv.at[pl.ds(0, 2)], IN_CV)
+
+    @pl.when(g == 0)
+    def _():
+        arrived(pr0, IN_PR0)
+        loop(0, bands, lambda m: home_out(m, pr0, 0))
 
     @pl.when(even)
     def _():
@@ -237,11 +246,6 @@
             pass_on(visitor(0, k), 0, k, below)
             came(1, k)
             pass_on(visitor(1, k), 2, k, above)
-
-    @pl.when(g == 0)
-    def _():
-        arrived(pr0, IN_PR0)
-        loop(0, bands, lambda m: home_out(m, pr0, 0))
 
     @pl.when(jnp.logical_not(even))
     def _():
@@ -283,12 +287,8 @@
         arrived(pr0, IN_PR0)
         arrived(pr1, IN_PR1)
         pl.semaphore_wait(turn, 1)
-
-        def both(m):
-            home_out(m, pr0, 0)
-            home_out(m, pr1, 1)
-
-        loop(0, bands, both)
+        loop(0, bands, lambda m: home_out(m, pr0, 0))
+        loop(0, bands, lambda m: home_out(m, pr1, 1))
 
     arrived(right_mat, IN_MAT)
     arrived(left_mat, IN_MAT)
@@ -356,22 +356,30 @@
             done[...] += term
 
     def slabs_out(m):
-        reach = nz // 2 - m // 2
-        tz = (z + jnp.where(m % 2 == 1, reach, nz - reach)) % nz
-        push(done.at[tz], ret_z.at[z // 2, z % 2], IN_Q, device(w, g, tz))
+        tz = far_first(m)
+        push(done.at[tz], ret_z.at[z // 2, z % 2], IN_Q + z // 2, device(w, g, tz), OUT_Q)
 
     loop(1, nz, slabs_out)
-    keep(done.at[z], ret_z.at[z // 2, z % 2], IN_Q)
-    arrived(ret_z, IN_Q)
-
-    def owners_out(d):
-        t = (place + d) % (2 * nw)
-        tw, tg = t // 2, t % 2
-        owner = (tw // 2) * 2 + tg
-        push(ret_z.at[owner, :, tw % 2], ret.at[:, g, :, w], IN_RET + g, device(tw, tg, z), IN_RET)
-
-    loop(1, 2 * nw, owners_out)
-    keep(ret_z.at[b, :, yh], ret.at[:, g, :, w], IN_RET + g)
+    keep(done.at[z], ret_z.at[z // 2, z % 2], IN_Q + z // 2)
+
+    def owner_out(m):
+        owner = (z // 2 + signed(m) + bands) % bands
+        arrived(ret_z.at[owner], IN_Q + owner)
+        dst = ret.at[:, g, :, w]
+        for part in range(2):
+            src = ret_z.at[owner, :, part]
+            here = jnp.logical_and(owner == b, yh == part)
+
+            @pl.when(here)
+            def _():
+                keep(src, dst, IN_RET + g)
+
+            @pl.when(jnp.logical_not(here))
+            def _():
+                target = {"band": owner, "slab": 2 * z + part}
+                push(src, dst, IN_RET + g, target, IN_RET)
+
+    loop(0, bands, owner_out)
     arrived(acc, IN_ACC)
     for core in range(2):
         arrived(ret.at[:, core], IN_RET + core)
@@ -406,7 +414,7 @@
         sent(vis.at[h, :, g], IN_VF + h)
         sent(tin.at[h, pl.ds(0, nw - 1)], IN_T + h)
         sent(tout.at[h, pl.ds(0, nw - 1)], IN_U + h)
-    sent(done.at[pl.ds(0, nz - 1)], IN_Q)
+    sent(done.at[pl.ds(0, nz - 1)], OUT_Q)
     sent(done.at[pl.ds(0, 2 * nw - 1)], IN_RET)
 
 
@@ -448,7 +456,7 @@
         scratch_shapes=[pltpu.VMEM(tiled, F32)]
         + [pltpu.VMEM((2 * extent, 2 * extent), BF16)] * 2
         + [pltpu.VMEM(shape, F32) for shape in scratch]
-        + [pltpu.SemaphoreType.DMA((N_SEM,))] * 2
+        + [pltpu.SemaphoreType.DMA((IN_Q + bands,))] * 2
         + [pltpu.SemaphoreType.REGULAR],
         compiler_params=pltpu.CompilerParams(
             collective_id=0, has_side_effects=True, vmem_limit_bytes=60 * 2**20

time: 168 us -> 158 us (0.940)
  Pallas kernels: 166 us -> 156 us
    pallas_call x1, Pallas kernels: 166 us -> 156 us  [body(): pl.pallas_call(functools.partial(kernel, bands, extent), out_shape=jax.Sh...]
where the time goes in v3:
time: 158 us
  Pallas kernels  156 us (99%)
  local copies, waits for them, and re-layouts  1.87 us (1%)
    pallas_call x1, Pallas kernels, body(): pl.pallas_call(functools.partial(kernel, bands, extent), out_shape=jax.Sh...  156 us

profile of v3, /device:TPU:1, one launch (start us, length us, event | category | flops | bytes accessed | tf_op | source)
XLA Modules:
  0.0 157.8 jit_solution(3092549577230327531)
XLA Ops:
  0.0 156.0 %shard_map.55 = f32[4,2,16,8,128]{4,3,2,1,0:T(8,128)} custom-call(f32[4,2,16,8,128]{4,3,2,1,0:T(8,128)} %bitcast.4, f32[4]{0:T(128)} %occ.1, f32[4,2,16,8,128]{4,3,2,1,0:T(8,128)} %bitcast.5, bf16[256,256]{1,0:T(8,128)(2,1)} %constant.4.clone.right_hbm, bf16[256,256]{1,0:T(8,128)(2,1)} %constant.5.clone.left_hbm), custom_call_target="tpu_custom_call" | custom-call | tf_op jit(solution)/shard_map/pallas_call | solution.py:451
  156.0 1.9 %copy.7 = f32[4,2,128,128]{3,2,1,0:T(8,128)} copy(f32[4,2,128,128]{3,2,1,0:T(8,128)} %bitcast.3) | data formatting | bytes 1048576

commit v4 on v3

--- a/solution.py
+++ b/solution.py
@@ -15,7 +15,7 @@
 BF16 = jnp.bfloat16
 SUB = 8
 
-CHUNKS = 4
+CHUNKS = 8
 
 IN_PV, IN_PR0, IN_PR1, IN_OCC, IN_CV, IN_R = range(6)
 IN_VF, IN_T, IN_U, IN_RET, OUT_Q, IN_ACC, IN_MAT, OUT_CHAIN = 6, 9, 12, 15, 17, 18, 19, 20

time: 158 us -> 158 us (level)
  no operation moved by 1% of the time
where the time goes in v4:
time: 158 us
  Pallas kernels  156 us (99%)
  local copies, waits for them, and re-layouts  1.87 us (1%)
    pallas_call x1, Pallas kernels, body(): pl.pallas_call(functools.partial(kernel, bands, extent), out_shape=jax.Sh...  156 us

profile of v4, /device:TPU:1, one launch (start us, length us, event | category | flops | bytes accessed | tf_op | source)
XLA Modules:
  0.0 157.6 jit_solution(10733995273711240999)
XLA Ops:
  0.0 155.8 %shard_map.55 = f32[4,2,16,8,128]{4,3,2,1,0:T(8,128)} custom-call(f32[4,2,16,8,128]{4,3,2,1,0:T(8,128)} %bitcast.4, f32[4]{0:T(128)} %occ.1, f32[4,2,16,8,128]{4,3,2,1,0:T(8,128)} %bitcast.5, bf16[256,256]{1,0:T(8,128)(2,1)} %constant.4.clone.right_hbm, bf16[256,256]{1,0:T(8,128)(2,1)} %constant.5.clone.left_hbm), custom_call_target="tpu_custom_call" | custom-call | tf_op jit(solution)/shard_map/pallas_call | solution.py:451
  155.8 1.9 %copy.7 = f32[4,2,128,128]{3,2,1,0:T(8,128)} copy(f32[4,2,128,128]{3,2,1,0:T(8,128)} %bitcast.3) | data formatting | bytes 1048576
